TPU v7x, 256 devices: a whole 4x4x8 slice. The times are simulated.
256 devices in a mesh: depth: 32 (over y_hi, z, core), res: 8 (over y_lo, x).
Axes of the slice: x: 4, y: 4 (y_hi: 2, y_lo: 2; y = y_hi * 2 + y_lo), z: 8, core: 2. Of those that a mesh axis runs over, the one named last changes fastest.
Arguments:
- alignment: bfloat16 [256, 512, 768], P('depth', 'res')
- seq_mask: int32 [256], P('depth'), may hold values from 0 to 1, as said below
- res_mask: int32 [512], P('res'), may hold values from 0 to 1, as said below
- row_query: bfloat16 [768, 768], replicated
- row_key: bfloat16 [768, 768], replicated, may hold values from -0.21875 to 0.21875
- row_value: bfloat16 [768, 768], replicated, may hold values from -0.21875 to 0.21875
- row_out: bfloat16 [768, 768], replicated, may hold values from -0.21875 to 0.21875
- col_query: bfloat16 [768, 768], replicated
- col_key: bfloat16 [768, 768], replicated, may hold values from -0.21875 to 0.21875
- col_value: bfloat16 [768, 768], replicated, may hold values from -0.21875 to 0.21875
- col_out: bfloat16 [768, 768], replicated, may hold values from -0.21875 to 0.21875
Outputs:
- layer_out: bfloat16 [256, 512, 768], P('depth', 'res')
Inputs may be any that keep to these rules, and one draw needn't show every extreme that they name: `seq_mask`: 0 marks a padded sequence; sequence 0 is never padded. `res_mask`: 0 marks a padded position; position 0 is never padded.
All inputs are finite; a program needn't handle non-finite values.
Results may differ from a plain program's by a relative error of at most 0.013.
Values may be sent and summed in bfloat16 or wider, within the bound.
A program may use at most 128 MiB of HBM per device.

v0:
```python
import math

import jax
import jax.numpy as jnp
from jax import lax
from jax.sharding import PartitionSpec as P

HEADS = 12


def layer_norm(values):
    wide = values.astype(jnp.float32)
    center = jnp.mean(wide, axis=-1, keepdims=True)
    spread = jnp.mean(jnp.square(wide - center), axis=-1, keepdims=True)
    return ((wide - center) * lax.rsqrt(spread + 1e-05)).astype(jnp.bfloat16)


def masked_softmax(scores, live_mask):
    alive = live_mask > 0
    largest = jnp.max(jnp.where(alive, scores, -jnp.inf), axis=-1, keepdims=True)
    raised = jnp.where(alive, jnp.exp(scores - largest), 0.0)
    return (raised / jnp.sum(raised, axis=-1, keepdims=True)).astype(jnp.bfloat16)


def body(
    alignment,
    seq_mask,
    res_mask,
    row_query,
    row_key,
    row_value,
    row_out,
    col_query,
    col_key,
    col_value,
    col_out,
):
    seq_rows, res_cols, width = alignment.shape
    head_dim = width // HEADS
    depth_size = lax.axis_size("depth")
    total_seqs = seq_rows * depth_size
    normed = layer_norm(alignment)
    seq_live = seq_mask.astype(jnp.float32)
    row_scale = head_dim ** (-0.5) / math.sqrt(total_seqs)
    queries = (
        jnp.dot(normed, row_query, preferred_element_type=jnp.float32)
        * row_scale
        * seq_live[:, None, None]
    ).astype(jnp.bfloat16)
    keys_local = jnp.dot(normed, row_key, preferred_element_type=jnp.float32).astype(jnp.bfloat16)
    values_local = jnp.dot(normed, row_value, preferred_element_type=jnp.float32).astype(
        jnp.bfloat16
    )
    query_heads = queries.reshape(seq_rows, res_cols, HEADS, head_dim)
    res_live = res_mask.astype(jnp.bfloat16)
    keys_all, values_all, live_all = (
        lax.all_gather(keys_local, "res", axis=1, tiled=True),
        lax.all_gather(values_local, "res", axis=1, tiled=True),
        lax.all_gather(res_live, "res", axis=0, tiled=True),
    )
    key_heads = keys_all.reshape(seq_rows, keys_all.shape[1], HEADS, head_dim)
    partial_value = jnp.einsum(
        "rihe,rjhe->hij", query_heads, key_heads, preferred_element_type=jnp.float32
    )
    tied = lax.psum(partial_value, "depth")
    row_weights = masked_softmax(tied, live_all)
    value_heads = values_all.reshape(seq_rows, values_all.shape[1], HEADS, head_dim)
    attended = jnp.einsum(
        "hij,rjhe->rihe", row_weights, value_heads, preferred_element_type=jnp.float32
    )
    row_mixed = attended.astype(jnp.bfloat16).reshape(seq_rows, res_cols, width)
    after_rows = (
        alignment.astype(jnp.float32)
        + jnp.dot(row_mixed, row_out, preferred_element_type=jnp.float32)
    ).astype(jnp.bfloat16)
    normed_cols = layer_norm(after_rows)
    per_peer = res_cols // depth_size
    grouped = normed_cols.reshape(seq_rows, depth_size, per_peer, width)
    live_grouped = jnp.broadcast_to(
        seq_mask.astype(jnp.bfloat16)[:, None, None], (seq_rows, depth_size, per_peer)
    )
    gathered = lax.all_to_all(grouped, "depth", split_axis=1, concat_axis=0, tiled=True)
    live_rows = lax.all_to_all(live_grouped, "depth", split_axis=1, concat_axis=0, tiled=True)
    columns = gathered[:, 0]
    all_rows = columns.shape[0]
    count = columns.shape[1]
    shape4 = (all_rows, count, HEADS, head_dim)
    col_queries = (
        (jnp.dot(columns, col_query, preferred_element_type=jnp.float32) * head_dim ** (-0.5))
        .astype(jnp.bfloat16)
        .reshape(shape4)
    )
    col_keys = (
        jnp.dot(columns, col_key, preferred_element_type=jnp.float32)
        .astype(jnp.bfloat16)
        .reshape(shape4)
    )
    col_values = (
        jnp.dot(columns, col_value, preferred_element_type=jnp.float32)
        .astype(jnp.bfloat16)
        .reshape(shape4)
    )
    scores = jnp.einsum(
        "rche,sche->chrs", col_queries, col_keys, preferred_element_type=jnp.float32
    )
    weights_col = masked_softmax(scores, live_rows[:, 0, 0])
    mixed = jnp.einsum(
        "chrs,sche->rche", weights_col, col_values, preferred_element_type=jnp.float32
    ).astype(jnp.bfloat16)
    col_mixed = mixed.reshape(all_rows, count, width)[:, None]
    returned = lax.all_to_all(col_mixed, "depth", split_axis=0, concat_axis=1, tiled=True).reshape(
        seq_rows, res_cols, width
    )
    return (
        after_rows.astype(jnp.float32)
        + jnp.dot(returned, col_out, preferred_element_type=jnp.float32)
    ).astype(jnp.bfloat16)


def solution(mesh):
    placed = (P("depth", "res", None), P("depth"), P("res"), P(), P(), P(), P(), P(), P(), P(), P())
    return jax.shard_map(
        body, mesh=mesh, in_specs=placed, out_specs=P("depth", "res", None), check_vma=False
    )
```

profile of v0, /device:TPU:2, one launch (start us, length us, event | category | flops | bytes accessed | tf_op | source)
XLA Modules:
  0.0 547.5 jit_solution(8621162949255780231)
XLA Ops:
  6.5 1.4 convert_reduce_fusion.1
  8.0 1.5 fusion.21
  9.5 3.1 convolution_convert_fusion.2
  12.7 0.0 all-gather.5.cloned.1.call-update
  12.7 0.0 all-gather.3.cloned.1.call-start
  12.8 1.8 convolution_convert_fusion.3
  14.5 0.0 all-gather.3.cloned.1.call-update
  14.5 0.0 all-reduce.3.cloned.1.call-start
  14.6 3.0 multiply_convert_fusion.1
  17.6 2.7 reshape.62
  20.3 68.0 %all-gather.5.cloned.1.call-done = bf16[8,512,768]{2,1,0:T(8,128)(2,1)} async-done(((bf16[8,64,768]{2,1,0:T(8,128)(2,1)}), bf16[8,512,768]{2,1,0:T(8,128)(2,1)}) %all-gather.5.cloned.1.call-update) | async-done | bytes 6291472 | tf_op jit(solution)/shard_map/all_gather | solution.py:57
  88.4 8.7 %copy.35 = bf16[8,512,768]{1,2,0:T(8,128)(2,1)} copy(bf16[8,512,768]{2,1,0:T(8,128)(2,1)} %all-gather.5.cloned.1.call-done) | data formatting | bytes 12582912 | tf_op jit(solution)/shard_map/all_gather | solution.py:57
  97.1 5.2 fusion.29
  102.3 0.0 all-reduce.3.cloned.1.call-update
  102.3 0.6 broadcast_in_dim.42
  102.9 9.8 %all-to-all-start.1 = ((bf16[8,32,2]{0,2,1:T(2,128)(2,1)}), bf16[8,32,2]{0,2,1:T(2,128)(2,1)S(1)}, u32[]{:S(2)}, u32[]{:S(2)}) async-start(bf16[8,32,2]{0,2,1:T(2,128)(2,1)} %broadcast_in_dim.42), calls=%async_computation.1 | async-start | bytes 32768 | tf_op jit(solution)/shard_map/all_to_all | solution.py:83
  112.8 0.7 dynamic-slice
  114.2 0.2 dynamic-update-slice
  114.4 18.8 %all-reduce = bf16[512]{0:T(512)(128)(2,1)S(1)} all-reduce(bf16[512]{0:T(512)(128)(2,1)S(1)} %dynamic-update-slice), channel_id=1, replica_groups=mesh['depth'=32,'res'=8] {'res'}, use_global_device_ids=true, to_apply=%add | all-reduce | flops 512 | bytes 2048
  133.3 30.8 %all-gather.3.cloned.1.call-done = bf16[8,512,768]{2,1,0:T(8,128)(2,1)} async-done(((bf16[8,64,768]{2,1,0:T(8,128)(2,1)}), bf16[8,512,768]{2,1,0:T(8,128)(2,1)}) %all-gather.3.cloned.1.call-update) | async-done | bytes 6291472 | tf_op jit(solution)/shard_map/all_gather | solution.py:58
  164.1 8.7 %copy.34 = bf16[8,512,768]{1,2,0:T(8,128)(2,1)} copy(bf16[8,512,768]{2,1,0:T(8,128)(2,1)} %all-gather.3.cloned.1.call-done) | data formatting | bytes 12582912 | tf_op jit(solution)/shard_map/all_gather | solution.py:58
  172.8 264.5 %all-reduce.3.cloned.1.call-done = f32[12,64,512]{2,1,0:T(8,128)} async-done(((f32[12,64,512]{2,1,0:T(8,128)}), f32[12,64,512]{2,1,0:T(8,128)}) %all-reduce.3.cloned.1.call-update) | async-done | bytes 1572880 | tf_op jit(solution)/shard_map/psum | solution.py:65
  437.3 2.4 fusion.62
  439.7 5.8 %fusion.34 = bf16[8,64,12,64]{1,3,0,2:T(8,128)(2,1)} fusion(bf16[8,512,12,64]{1,3,2,0:T(8,128)(2,1)} %bitcast.76, f32[12,64,512]{2,1,0:T(8,128)S(1)} %get-tuple-element.6, f32[12,64]{1,0:T(8,128)S(1)} %get-tuple-element.5), kind=kOutput, calls=%fused_computation.38 | convolution fusion | flops 403832832 | bytes 8653824 | tf_op jit(solution)/shard_map/hij,rjhe->rihe/dot_general | solution.py:68
  445.5 3.5 copy.39
  449.0 2.0 reshape.64
  451.1 2.2 convert_reduce_fusion
  453.3 0.3 fusion.19
  453.7 0.3 fusion.20
  453.9 0.3 reshape.65
  454.2 1.4 copy.40
  455.7 7.4 %all-to-all-start = ((bf16[8,32,2,768]{3,2,0,1:T(2,128)(2,1)}), bf16[8,32,2,768]{3,2,0,1:T(2,128)(2,1)S(1)}, u32[]{:S(2)}, u32[]{:S(2)}) async-start(bf16[8,32,2,768]{3,2,0,1:T(2,128)(2,1)} %copy.40), calls=%async_computation | async-start | bytes 1572864 | tf_op jit(solution)/shard_map/all_to_all | solution.py:82
  463.1 0.1 all_to_all.41
  463.2 24.5 %all-to-all-done = bf16[8,32,2,768]{3,2,0,1:T(2,128)(2,1)S(1)} async-done(((bf16[8,32,2,768]{3,2,0,1:T(2,128)(2,1)}), bf16[8,32,2,768]{3,2,0,1:T(2,128)(2,1)S(1)}, u32[]{:S(2)}, u32[]{:S(2)}) %all-to-all-start) | async-done | bytes 786464 | tf_op jit(solution)/shard_map/all_to_all | solution.py:82
  487.8 2.0 multiply_convert_fusion
  489.8 0.3 copy.44
  490.1 2.9 convolution_convert_fusion
  493.0 1.4 copy.45
  494.4 2.9 convolution_convert_fusion.1
  497.4 1.4 copy.42
  498.8 5.6 %fusion.63 = (f32[2,12,256]{2,1,0:T(8,128)S(1)}, f32[2,12,256,256]{2,3,1,0:T(8,128)}) fusion(pred[256]{0:T(512)(128)(4,1)S(1)} %compare_reduce_fusion, bf16[256,2,12,64]{0,3,2,1:T(8,128)(2,1)S(1)} %bitcast.82, bf16[256,2,12,64]{0,3,2,1:T(8,128)(2,1)S(1)} %bitcast.83), kind=kOutput, calls=%fused_computation.73 | convolution fusion | flops 408944896 | bytes 7889152 | tf_op jit(solution)/shard_map/sub | solution.py:21
  504.4 3.5 fusion.37
  507.8 0.8 copy.47
  508.7 28.1 %all_to_all.48 = bf16[256,1,2,768]{3,2,1,0:T(2,128)(2,1)S(1)} all-to-all(bf16[256,1,2,768]{3,2,1,0:T(2,128)(2,1)S(1)} %copy.47), channel_id=1, replica_groups=mesh['depth'=32,'res'=8] {'depth'}, dimensions={0} | all-to-all | bytes 1572864 | tf_op jit(solution)/shard_map/all_to_all | solution.py:111
  536.8 0.1 copy.80
  536.9 0.8 copy.49
  537.7 0.3 reshape.69
  538.0 3.0 fusion.24
  (27 shorter events, 0.1 us)
Async XLA Ops:
  6.5 444.5 %copy-start = (bf16[768,768]{1,0:T(8,128)(2,1)S(1)}, bf16[768,768]{1,0:T(8,128)(2,1)}, u32[]{:S(2)}) copy-start(bf16[768,768]{1,0:T(8,128)(2,1)} %param.17) | copy-start | bytes 3538948
  6.5 3.0 copy-start.2
  6.5 81.8 %all-gather.5.cloned.1.call-start = ((), (), s32[]{:S(2)}) async-start(), calls=%async_computation.4 | async-start | bytes 7077888 | tf_op jit(solution)/shard_map/all_gather | solution.py:57
  9.5 3.2 copy-start.3
  12.7 1.9 copy-start.4
  12.7 151.4 %all-gather.3.cloned.1.call-start = ((), (), s32[]{:S(2)}) async-start(), calls=%async_computation.3 | async-start | bytes 7077888 | tf_op jit(solution)/shard_map/all_gather | solution.py:58
  14.5 422.7 %all-reduce.3.cloned.1.call-start = ((), (), s32[]{:S(2)}) async-start(), calls=%async_computation.5 | async-start | bytes 3145728 | tf_op jit(solution)/shard_map/psum | solution.py:65
  102.3 10.5 %copy-start.5 = (s32[64]{0:T(128)S(1)}, s32[64]{0:T(128)}, u32[]{:S(2)}) copy-start(s32[64]{0:T(128)} %param.13) | copy-start | bytes 772
  102.3 10.5 %copy-start.6 = (u32[256]{0:T(256)S(1)}, u32[256]{0:T(256)}, u32[]{:S(2)}) copy-start(u32[256]{0:T(256)} %constant.23) | copy-start | bytes 3076
  102.9 352.7 %all-to-all-start.1 = ((bf16[8,32,2]{0,2,1:T(2,128)(2,1)}), bf16[8,32,2]{0,2,1:T(2,128)(2,1)S(1)}, u32[]{:S(2)}, u32[]{:S(2)}) async-start(bf16[8,32,2]{0,2,1:T(2,128)(2,1)} %broadcast_in_dim.42), calls=%async_computation.1 | async-start | bytes 32768 | tf_op jit(solution)/shard_map/all_to_all | solution.py:83
  455.7 32.1 %all-to-all-start = ((bf16[8,32,2,768]{3,2,0,1:T(2,128)(2,1)}), bf16[8,32,2,768]{3,2,0,1:T(2,128)(2,1)S(1)}, u32[]{:S(2)}, u32[]{:S(2)}) async-start(bf16[8,32,2,768]{3,2,0,1:T(2,128)(2,1)} %copy.40), calls=%async_computation | async-start | bytes 1572864 | tf_op jit(solution)/shard_map/all_to_all | solution.py:82
  537.7 3.3 copy-start.1
Sparse Core Ops, SparseCore 0:
  12.8 75.5 all-gather.4
  90.2 73.8 all-gather.2
  166.7 270.4 all-reduce.2
where the time goes:
time: 549 us; the launch traced here: 548 us
  waiting for transfers between devices  388 us (71%)
  blocking collectives  46.9 us (9%)
  matrix products  41.1 us (7%)
  local copies, waits for them, and re-layouts  34.1 us (6%)
  starting transfers between devices  17.4 us (3%)
  between operations  14.1 us (3%)
  other arithmetic  6.04 us (1%)
    psum x1, waiting for transfers between devices, body(): tied = lax.psum(partial_value, 'depth')  264 us
    all_gather x1, waiting for transfers between devices, body(): lax.all_gather(keys_local, 'res', axis=1, tiled=True)  68 us
    all_gather x1, waiting for transfers between devices, body(): lax.all_gather(values_local, 'res', axis=1, tiled=True)  30.8 us
    all_to_all x1, blocking collectives, body(): lax.all_to_all(col_mixed, 'depth', split_axis=0, concat_axis=1, tiled=True)  28.1 us
    all_to_all x1, waiting for transfers between devices, body(): lax.all_to_all(grouped, 'depth', split_axis=1, concat_axis=0, tiled=True)  24.5 us
    unnamed x1, blocking collectives  18.8 us
  transfers between devices with their start and end apart: 5, of which 4 were waited for; matrix products, arithmetic and copies ran while one was open for 9% of the time, Pallas kernels for 0%

commit v1 on v0

v1 whole, which is shorter than its diff:
```python
import functools
import math

import jax
import jax.numpy as jnp
from jax import lax
from jax.experimental import pallas as pl
from jax.experimental.pallas import tpu as pltpu
from jax.sharding import PartitionSpec as P

HEAD = 64
LANES = 128
F32 = jnp.float32
BF16 = jnp.bfloat16
MESH = pl.DeviceIdType.MESH


class Shape:
    def __init__(self, y_hi=2, z=8, core=2, y_lo=2, x=4, seqs=8, spots=64, width=768):
        self.y_hi, self.z, self.core, self.y_lo, self.x = y_hi, z, core, y_lo, x
        self.seqs, self.spots, self.width = seqs, spots, width
        self.depth = y_hi * z * core
        self.res = y_lo * x
        self.y = y_hi * y_lo
        self.heads = width // HEAD
        self.group = self.heads // x
        self.part = seqs // y_lo
        self.wide = self.part * HEAD
        self.all_spots = self.res * spots
        self.tied_rows = self.group * self.all_spots
        self.half = self.all_spots // core
        self.block = self.tied_rows // (self.z * self.y)
        self.rows = seqs * spots
        self.per = spots // self.depth
        self.msg = self.per * seqs
        self.up = self.z // 2
        self.down = (self.z - 1) // 2


def remote(src, dst, send, recv, device):
    return pltpu.make_async_remote_copy(
        src_ref=src, dst_ref=dst, send_sem=send, recv_sem=recv, device_id=device, device_id_type=MESH
    )


def normalise(wide):
    center = jnp.mean(wide, axis=-1, keepdims=True)
    moved = wide - center
    spread = jnp.mean(jnp.square(moved), axis=-1, keepdims=True)
    return moved * lax.rsqrt(spread + 1e-05)


def nt_dot(a, b):
    return lax.dot_general(a, b, (((1,), (1,)), ((), ())), preferred_element_type=F32)


def dot(a, b):
    return jnp.dot(a, b, preferred_element_type=F32)


def low_half(shape):
    return lax.broadcasted_iota(jnp.int32, shape, len(shape) - 1) % LANES < HEAD


def swap_halves(first, second):
    low = low_half(first.shape)
    return (
        jnp.where(low, first, pltpu.roll(second, HEAD, 1)),
        jnp.where(low, pltpu.roll(first, HEAD, 1), second),
    )


def chunk_of(total, limit):
    size = min(total, limit)
    while total % size:
        size //= 2
    return size


def row_kernel(
    sh,
    x_ref,
    marks_ref,
    wq_ref,
    wk_ref,
    wv_ref,
    wo_ref,
    after_ref,
    perm_ref,
    seqs_ref,
    normed,
    send_k,
    send_q,
    send_v,
    got_k,
    got_q,
    got_v,
    res_marks,
    tied,
    pair,
    up_buf,
    down_buf,
    y1_src,
    y1_buf,
    y2_buf,
    z2_src,
    z2_buf,
    own,
    other,
    weights,
    mixed,
    back,
    gathered,
    mark_send,
    mark_recv,
    res_send,
    res_recv,
    qkv_send,
    qkv_recv,
    local_sem,
    pair_send,
    pair_recv,
    up_send,
    up_recv,
    down_send,
    down_recv,
    y_send,
    y_recv,
    z_send,
    z_recv,
    gup_send,
    gup_recv,
    gdown_send,
    gdown_recv,
    back_send,
    back_recv,
):
    d = lax.axis_index("depth")
    m = lax.axis_index("res")
    core = d % sh.core
    z = (d // sh.core) % sh.z
    y_hi = d // (sh.core * sh.z)
    x = m % sh.x
    y_lo = m // sh.x
    y = y_hi * sh.y_lo + y_lo
    mate = 1 - core

    def at_depth(k):
        return (
            ((y_hi + k // (sh.z * sh.core)) % sh.y_hi) * (sh.z * sh.core)
            + ((z + (k // sh.core) % sh.z) % sh.z) * sh.core
            + (core + k % sh.core) % sh.core
        )

    def at_res(k):
        return ((y_lo + k // sh.x) % sh.y_lo) * sh.x + (x + k % sh.x) % sh.x

    def at_z(k):
        return (y_hi * sh.z + (z + k + sh.z) % sh.z) * sh.core + core

    def at_y(k):
        there = (y + k) % sh.y
        return ((there // sh.y_lo) * sh.z + z) * sh.core + core, (there % sh.y_lo) * sh.x + x, there

    mate_id = ((y_hi * sh.z + z) * sh.core + mate, m)

    barrier = pltpu.get_barrier_semaphore()

    def greet_depth(k, c):
        pl.semaphore_signal(barrier, inc=1, device_id=(at_depth(k), m), device_id_type=MESH)
        return c

    lax.fori_loop(1, sh.depth, greet_depth, 0)

    def greet_res(k, c):
        pl.semaphore_signal(barrier, inc=1, device_id=(d, at_res(k)), device_id_type=MESH)
        return c

    lax.fori_loop(1, sh.res, greet_res, 0)
    for k in range(1, sh.y):
        dy, ry, _ = at_y(k)
        pl.semaphore_signal(barrier, inc=1, device_id=(dy, ry), device_id_type=MESH)
    pl.semaphore_wait(barrier, sh.depth - 1 + sh.res - 1 + sh.y - 1)

    seqs_ref[pl.ds(d, 1)] = marks_ref[1:2]
    res_marks[pl.ds(m, 1)] = marks_ref[0:1]

    def mark_copy(k):
        return remote(
            marks_ref.at[1], seqs_ref.at[d], mark_send.at[k], mark_recv.at[k], (at_depth(k), m)
        )

    def res_copy(k):
        return remote(
            marks_ref.at[0], res_marks.at[m], res_send.at[k], res_recv.at[k], (d, at_res(k))
        )

    lax.fori_loop(1, sh.depth, lambda k, c: (mark_copy(k).start(), c)[1], 0)
    lax.fori_loop(1, sh.res, lambda k, c: (res_copy(k).start(), c)[1], 0)

    step = sh.spots

    def norm_rows(r, c):
        rows = pl.ds(pl.multiple_of(r * step, step), step)
        normed[rows, :] = normalise(x_ref[rows, :].astype(F32)).astype(BF16)
        return c

    lax.fori_loop(0, sh.seqs, norm_rows, 0)

    part_rows = sh.part * sh.spots
    ncol = chunk_of(sh.width, 256)

    def project(w_ref, out_ref, scale):
        def half(s, c):
            rows = pl.ds(pl.multiple_of(s * part_rows, part_rows), part_rows)
            for n in range(sh.width // ncol):
                res = dot(normed[rows, :], w_ref[:, n * ncol : (n + 1) * ncol])
                tiles = []
                for r in range(sh.part):
                    t = res[r * sh.spots : (r + 1) * sh.spots]
                    if scale is not None:
                        live = marks_ref[1, pl.ds(s * sh.part + r, 1), :]
                        t = t * (jnp.tile(live, (1, ncol // LANES)) * scale)
                    tiles.append(t)
                for p in range(ncol // LANES):
                    lanes = slice(p * LANES, (p + 1) * LANES)
                    head = (n * ncol + p * LANES) // HEAD
                    for rp in range(sh.part // 2):
                        even, odd = swap_halves(tiles[2 * rp][:, lanes], tiles[2 * rp + 1][:, lanes])
                        to = slice(rp * LANES, (rp + 1) * LANES)
                        for h, t in ((head, even), (head + 1, odd)):
                            out_ref[s * sh.x + h // sh.group, h % sh.group, :, to] = t.astype(BF16)
            return c

        lax.fori_loop(0, sh.y_lo, half, 0)

    def qkv_copy(i, src, dst, k):
        there = at_res(k)
        return remote(
            src.at[there], dst.at[:, m], qkv_send.at[i, k], qkv_recv.at[i, k], (d, there)
        )

    def own_copy(i, src, dst):
        return pltpu.make_async_copy(src.at[m], dst.at[:, m], local_sem.at[i])

    sets = ((0, send_k, got_k, wk_ref, None), (1, send_q, got_q, wq_ref, None), (2, send_v, got_v, wv_ref, None))
    row_scale = HEAD ** (-0.5) / math.sqrt(sh.depth * sh.seqs)
    for i, src, dst, w_ref, _ in sets:
        project(w_ref, src, row_scale if i == 1 else None)
        own_copy(i, src, dst).start()
        lax.fori_loop(1, sh.res, lambda k, c: (qkv_copy(i, src, dst, k).start(), c)[1], 0)

    def arrive_qkv(i, src, dst):
        own_copy(i, src, dst).wait()

        def one(k, c):
            back_m = ((y_lo + sh.y_lo - k // sh.x) % sh.y_lo) * sh.x + (x + sh.x - k % sh.x) % sh.x
            remote(
                src.at[0], dst.at[:, back_m], qkv_send.at[i, k], qkv_recv.at[i, k], (d, back_m)
            ).wait_recv()
            return c

        lax.fori_loop(1, sh.res, one, 0)

    arrive_qkv(0, send_k, got_k)
    arrive_qkv(1, send_q, got_q)

    for h in range(sh.group):
        q = got_q[h].reshape(sh.all_spots, sh.wide)
        for j in range(sh.core):
            per_half = sh.res // sh.core
            k = got_k[h, j * per_half : (j + 1) * per_half].reshape(sh.half, sh.wide)
            res = nt_dot(q, k)
            zs = sh.z * sh.y // sh.group
            tied[j, h * sh.all_spots : (h + 1) * sh.all_spots, :] = res

    half_copy = remote(tied.at[mate], pair, pair_send.at[0], pair_recv.at[0], mate_id)
    half_copy.start()
    half_copy.wait_recv()
    rows_z = sh.y * sh.block
    tied_step = sh.block

    def add_pair(t, c):
        rows = pl.ds(pl.multiple_of(t * tied_step, tied_step), tied_step)
        pair[rows, :] = pair[rows, :] + tied[core, rows, :]
        return c

    lax.fori_loop(0, sh.tied_rows // tied_step, add_pair, 0)

    low = pl.ds(0, LANES)
    high = pl.ds(LANES, LANES)

    def z_rows(k):
        return pl.ds(pl.multiple_of(((z + k + sh.z) % sh.z) * rows_z, rows_z), rows_z)

    def block_rows(zz, yy):
        return pl.ds(pl.multiple_of(zz * rows_z + yy * sh.block, sh.block), sh.block)

    def y2_copies(k):
        dy, ry, there = at_y(k)
        return [
            remote(
                pair.at[block_rows(zz, there), high],
                y2_buf.at[k - 1, zz],
                y_send.at[0, k, zz],
                y_recv.at[0, k, zz],
                (dy, ry),
            )
            for zz in range(sh.z)
        ]

    def up_copy(t):
        src = pair.at[z_rows(sh.up), low] if t == 0 else up_buf.at[t - 1]
        return remote(src, up_buf.at[t], up_send.at[t], up_recv.at[t], (at_z(1), m))

    def down_copy(t):
        src = pair.at[z_rows(-sh.down), low] if t == 0 else down_buf.at[t - 1]
        return remote(src, down_buf.at[t], down_send.at[t], down_recv.at[t], (at_z(-1), m))

    def z2_copy(k):
        there = (z + k) % sh.z
        return remote(
            z2_src.at[there], z2_buf.at[k - 1], z_send.at[0, k], z_recv.at[0, k], (at_z(k), m)
        )

    def y1_copy(k):
        dy, ry, there = at_y(k)
        return remote(
            y1_src.at[there], y1_buf.at[k - 1], y_send.at[1, k, 0], y_recv.at[1, k, 0], (dy, ry)
        )

    up_copy(0).start()
    if sh.down:
        down_copy(0).start()
    for k in range(1, sh.y):
        for c in y2_copies(k):
            c.start()
    for t in range(1, sh.up):
        up_copy(t - 1).wait_recv()
        up_buf[t - 1] = up_buf[t - 1] + pair[z_rows(sh.up - t), low]
        up_copy(t).start()
        if t < sh.down:
            down_copy(t - 1).wait_recv()
            down_buf[t - 1] = down_buf[t - 1] + pair[z_rows(t - sh.down), low]
            down_copy(t).start()
    for k in range(1, sh.y):
        for c in y2_copies(k):
            c.wait_recv()
    for zz in range(sh.z):
        total = pair[block_rows(zz, y), high]
        for k in range(1, sh.y):
            total = total + y2_buf[k - 1, zz]
        z2_src[zz] = total
    for k in range(1, sh.z):
        z2_copy(k).start()
    up_copy(sh.up - 1).wait_recv()
    if sh.down:
        down_copy(sh.down - 1).wait_recv()
    total = pair[z_rows(0), low] + up_buf[sh.up - 1]
    if sh.down:
        total = total + down_buf[sh.down - 1]
    y1_src[...] = total.reshape(sh.y, sh.block, LANES)
    for k in range(1, sh.y):
        y1_copy(k).start()
    for k in range(1, sh.y):
        y1_copy(k).wait_recv()
    total = y1_src[y]
    for k in range(1, sh.y):
        total = total + y1_buf[k - 1]
    own[:, 0:LANES] = total
    for k in range(1, sh.z):
        z2_copy(k).wait_recv()
    total = z2_src[z]
    for k in range(1, sh.z):
        total = total + z2_buf[k - 1]
    own[:, LANES : 2 * LANES] = total

    own_pair = remote(own, other, pair_send.at[1], pair_recv.at[1], mate_id)
    own_pair.start()

    def res_arrive(k, c):
        back_m = ((y_lo + sh.y_lo - k // sh.x) % sh.y_lo) * sh.x + (x + sh.x - k % sh.x) % sh.x
        remote(
            marks_ref.at[0], res_marks.at[back_m], res_send.at[k], res_recv.at[k], (d, back_m)
        ).wait_recv()
        return c

    lax.fori_loop(1, sh.res, res_arrive, 0)

    def live_columns(which):
        per_half = sh.res // sh.core
        tiles = []
        for p in range(per_half // 2):
            first = res_marks[which * per_half + 2 * p]
            second = res_marks[which * per_half + 2 * p + 1]
            tiles.append(jnp.where(low_half(first.shape), first, second))
        return jnp.concatenate(tiles, axis=1)[0:1]

    own_live = live_columns(core) > 0.0
    other_live = live_columns(mate) > 0.0
    own_pair.wait_recv()
    own_s = jnp.where(own_live, own[...], -jnp.inf)
    other_s = jnp.where(other_live, other[...], -jnp.inf)
    top = jnp.maximum(
        jnp.max(own_s, axis=-1, keepdims=True), jnp.max(other_s, axis=-1, keepdims=True)
    )
    own_e = jnp.exp(own_s - top)
    other_e = jnp.exp(other_s - top)
    sums = jnp.sum(own_e, axis=-1, keepdims=True) + jnp.sum(other_e, axis=-1, keepdims=True)
    weights[core, block_rows(z, y), :] = (own_e / sums).astype(BF16)

    def gz_copy(k, zz):
        rows = block_rows(zz, y)
        ref = weights.at[core, rows, low]
        return remote(ref, ref, z_send.at[1, k], z_recv.at[1, k], (at_z(k), m))

    def gy_copy(k, yy):
        dy, ry, _ = at_y(k)
        rows = block_rows(z, yy)
        ref = weights.at[core, rows, high]
        return remote(ref, ref, y_send.at[2, k, 0], y_recv.at[2, k, 0], (dy, ry))

    def gy_all(k, yy):
        dy, ry, _ = at_y(k)
        copies = []
        for zz in range(sh.z):
            ref = weights.at[core, block_rows(zz, yy), low]
            copies.append(remote(ref, ref, y_send.at[3, k, zz], y_recv.at[3, k, zz], (dy, ry)))
        return copies

    def gup_copy(t, came):
        ref = weights.at[core, z_rows(-t - came), high]
        return remote(ref, ref, gup_send.at[t], gup_recv.at[t], (at_z(1), m))

    def gdown_copy(t, came):
        ref = weights.at[core, z_rows(t + came), high]
        return remote(ref, ref, gdown_send.at[t], gdown_recv.at[t], (at_z(-1), m))

    for k in range(1, sh.y):
        gy_copy(k, y).start()
    for k in range(1, sh.z):
        gz_copy(k, z).start()
    for k in range(1, sh.y):
        gy_copy(k, (y + sh.y - k) % sh.y).wait_recv()
    gup_copy(0, 0).start()
    if sh.down:
        gdown_copy(0, 0).start()
    for k in range(1, sh.z):
        gz_copy(k, (z + sh.z - k) % sh.z).wait_recv()
    for k in range(1, sh.y):
        for c in gy_all(k, y):
            c.start()
    for t in range(1, sh.up):
        gup_copy(t - 1, 1).wait_recv()
        gup_copy(t, 0).start()
        if t < sh.down:
            gdown_copy(t - 1, 1).wait_recv()
            gdown_copy(t, 0).start()
    gup_copy(sh.up - 1, 1).wait_recv()
    if sh.down:
        gdown_copy(sh.down - 1, 1).wait_recv()
    for k in range(1, sh.y):
        for c in gy_all(k, (y + sh.y - k) % sh.y):
            c.wait_recv()
    weights_pair = remote(
        weights.at[core], weights.at[core], pair_send.at[2], pair_recv.at[2], mate_id
    )
    weights_pair.start()
    arrive_qkv(2, send_v, got_v)
    remote(
        weights.at[mate], weights.at[mate], pair_send.at[2], pair_recv.at[2], mate_id
    ).wait_recv()

    for h in range(sh.group):
        v = got_v[h].reshape(sh.all_spots, sh.wide)
        rows = slice(h * sh.all_spots, (h + 1) * sh.all_spots)
        total = dot(weights[0, rows, :], v[: sh.half])
        for j in range(1, sh.core):
            total = total + dot(weights[j, rows, :], v[j * sh.half : (j + 1) * sh.half])
        mixed[h] = total.astype(BF16).reshape(sh.res, sh.spots, sh.wide)

    def back_copy(k, there, here):
        return remote(
            mixed.at[:, there], back.at[here], back_send.at[k], back_recv.at[k], (d, there)
        )

    home = pltpu.make_async_copy(mixed.at[:, m], back.at[m], local_sem.at[3])
    home.start()
    lax.fori_loop(1, sh.res, lambda k, c: (back_copy(k, at_res(k), m).start(), c)[1], 0)
    home.wait()

    def back_arrive(k, c):
        back_m = ((y_lo + sh.y_lo - k // sh.x) % sh.y_lo) * sh.x + (x + sh.x - k % sh.x) % sh.x
        back_copy(k, back_m, back_m).wait_recv()
        return c

    lax.fori_loop(1, sh.res, back_arrive, 0)

    def unpack(s, c):
        for p in range(sh.heads // 2):
            for rp in range(sh.part // 2):
                lanes = slice(rp * LANES, (rp + 1) * LANES)
                tiles = []
                for h in (2 * p, 2 * p + 1):
                    tiles.append(
                        back[s * sh.x + h // sh.group, h % sh.group, :, lanes].astype(F32)
                    )
                first, second = swap_halves(*tiles)
                for r, t in ((0, first), (1, second)):
                    row = (s * sh.part + 2 * rp + r) * sh.spots
                    gathered[
                        pl.ds(pl.multiple_of(row, sh.spots), sh.spots), p * LANES : (p + 1) * LANES
                    ] = t.astype(BF16)
        return c

    lax.fori_loop(0, sh.y_lo, unpack, 0)

    def close_rows(s, c):
        rows = pl.ds(pl.multiple_of(s * part_rows, part_rows), part_rows)
        after = (x_ref[rows, :].astype(F32) + dot(gathered[rows, :], wo_ref[...])).astype(BF16)
        after_ref[rows, :] = after
        normed[rows, :] = normalise(after.astype(F32)).astype(BF16)
        return c

    lax.fori_loop(0, sh.y_lo, close_rows, 0)

    prow = chunk_of(sh.rows, 256)

    def permute(t, c):
        a = lax.broadcasted_iota(jnp.int32, (prow, sh.rows), 0) + t * prow
        b = lax.broadcasted_iota(jnp.int32, (prow, sh.rows), 1)
        pick = jnp.where(b == (a % sh.seqs) * sh.spots + a // sh.seqs, 1.0, 0.0).astype(BF16)
        perm_ref[pl.ds(pl.multiple_of(t * prow, prow), prow), :] = dot(pick, normed[...]).astype(BF16)
        return c

    lax.fori_loop(0, sh.rows // prow, permute, 0)

    def seqs_arrive(k, c):
        back_d = (
            ((y_hi + sh.y_hi - k // (sh.z * sh.core)) % sh.y_hi) * (sh.z * sh.core)
            + ((z + sh.z - (k // sh.core) % sh.z) % sh.z) * sh.core
            + (core + sh.core - k % sh.core) % sh.core
        )
        remote(
            marks_ref.at[1], seqs_ref.at[back_d], mark_send.at[k], mark_recv.at[k], (back_d, m)
        ).wait_recv()
        mark_copy(k).wait_send()
        return c

    lax.fori_loop(1, sh.depth, seqs_arrive, 0)

    def sent_res(k, c):
        res_copy(k).wait_send()
        for i, src, dst, _, _ in sets:
            qkv_copy(i, src, dst, k).wait_send()
        back_copy(k, at_res(k), m).wait_send()
        return c

    lax.fori_loop(1, sh.res, sent_res, 0)
    half_copy.wait_send()
    own_pair.wait_send()
    weights_pair.wait_send()
    for t in range(sh.up):
        up_copy(t).wait_send()
        gup_copy(t, 0).wait_send()
    for t in range(sh.down):
        down_copy(t).wait_send()
        gdown_copy(t, 0).wait_send()
    for k in range(1, sh.y):
        for c in y2_copies(k):
            c.wait_send()
        for c in gy_all(k, y):
            c.wait_send()
        y1_copy(k).wait_send()
        gy_copy(k, y).wait_send()
    for k in range(1, sh.z):
        z2_copy(k).wait_send()
        gz_copy(k, z).wait_send()


def column_kernel(
    sh,
    perm_ref,
    after_ref,
    seqs_ref,
    wq_ref,
    wk_ref,
    wv_ref,
    wo_ref,
    out_ref,
    rows_in,
    q_buf,
    k_buf,
    v_buf,
    wide,
    rows_out,
    rows_back,
    straight,
    in_send,
    in_recv,
    out_send,
    out_recv,
    local_sem,
):
    d = lax.axis_index("depth")
    m = lax.axis_index("res")
    core = d % sh.core
    z = (d // sh.core) % sh.z
    y_hi = d // (sh.core * sh.z)

    def at_depth(k):
        return (
            ((y_hi + k // (sh.z * sh.core)) % sh.y_hi) * (sh.z * sh.core)
            + ((z + (k // sh.core) % sh.z) % sh.z) * sh.core
            + (core + k % sh.core) % sh.core
        )

    def from_depth(k):
        return (
            ((y_hi + sh.y_hi - k // (sh.z * sh.core)) % sh.y_hi) * (sh.z * sh.core)
            + ((z + sh.z - (k // sh.core) % sh.z) % sh.z) * sh.core
            + (core + sh.core - k % sh.core) % sh.core
        )

    barrier = pltpu.get_barrier_semaphore()

    def greet(k, c):
        pl.semaphore_signal(barrier, inc=1, device_id=(at_depth(k), m), device_id_type=MESH)
        return c

    lax.fori_loop(1, sh.depth, greet, 0)
    pl.semaphore_wait(barrier, sh.depth - 1)

    def in_copy(k, there, here):
        return remote(
            perm_ref.at[there], rows_in.at[here], in_send.at[k], in_recv.at[k], (there, m)
        )

    own = pltpu.make_async_copy(perm_ref.at[d], rows_in.at[d], local_sem.at[0])
    own.start()
    lax.fori_loop(1, sh.depth, lambda k, c: (in_copy(k, at_depth(k), d).start(), c)[1], 0)
    own.wait()

    def in_arrive(k, c):
        in_copy(k, from_depth(k), from_depth(k)).wait_recv()
        return c

    lax.fori_loop(1, sh.depth, in_arrive, 0)

    seqs = sh.depth * sh.seqs
    rows = rows_in[...].reshape(sh.depth * sh.msg, sh.width)
    ncol = chunk_of(sh.width, 256)
    for w_ref, to, scale in ((wq_ref, q_buf, HEAD ** (-0.5)), (wk_ref, k_buf, None), (wv_ref, v_buf, None)):
        for n in range(sh.width // ncol):
            lanes = slice(n * ncol, (n + 1) * ncol)
            res = dot(rows, w_ref[:, lanes])
            if scale is not None:
                res = res * scale
            res = res.reshape(sh.depth, sh.per, sh.seqs, ncol)
            for p in range(sh.per):
                to[p, :, lanes] = res[:, p].reshape(seqs, ncol).astype(BF16)

    pick = jnp.where(
        lax.broadcasted_iota(jnp.int32, (8, LANES), 1) == 0, 1.0, 0.0
    ).astype(F32)
    alive = nt_dot(pick, seqs_ref[...].reshape(seqs, LANES))[0:1] > 0.5

    def attend(p, c):
        for pair in range(sh.heads // 2):
            lanes = slice(pair * LANES, (pair + 1) * LANES)
            q = q_buf[p, :, lanes]
            k = k_buf[p, :, lanes]
            v = v_buf[p, :, lanes]
            low = low_half(q.shape)
            halves = []
            for keep in (low, jnp.logical_not(low)):
                scores = nt_dot(jnp.where(keep, q, jnp.zeros_like(q)), k)
                scores = jnp.where(alive, scores, -jnp.inf)
                raised = jnp.exp(scores - jnp.max(scores, axis=-1, keepdims=True))
                share = (raised / jnp.sum(raised, axis=-1, keepdims=True)).astype(BF16)
                halves.append(dot(share, v))
            mixed = jnp.where(low, halves[0], halves[1])
            wide[:, p, :, lanes] = mixed.reshape(sh.depth, sh.seqs, LANES)
        return c

    lax.fori_loop(0, sh.per, attend, 0)
    rows_out[...] = wide[...].reshape(sh.depth, sh.msg, sh.width).astype(BF16)

    def out_copy(k, there, here):
        return remote(
            rows_out.at[there], rows_back.at[here], out_send.at[k], out_recv.at[k], (there, m)
        )

    own_back = pltpu.make_async_copy(rows_out.at[d], rows_back.at[d], local_sem.at[1])
    own_back.start()
    lax.fori_loop(1, sh.depth, lambda k, c: (out_copy(k, at_depth(k), d).start(), c)[1], 0)
    own_back.wait()

    def out_arrive(k, c):
        out_copy(k, from_depth(k), from_depth(k)).wait_recv()
        return c

    lax.fori_loop(1, sh.depth, out_arrive, 0)

    prow = chunk_of(sh.rows, 256)

    def finish(t, c):
        part = pl.ds(pl.multiple_of(t * prow, prow), prow)
        a = lax.broadcasted_iota(jnp.int32, (prow, sh.rows), 0) + t * prow
        b = lax.broadcasted_iota(jnp.int32, (prow, sh.rows), 1)
        pick = jnp.where(b == (a % sh.spots) * sh.seqs + a // sh.spots, 1.0, 0.0).astype(BF16)
        straight[part, :] = dot(pick, rows_back[...].reshape(sh.rows, sh.width)).astype(BF16)
        out_ref[part, :] = (
            after_ref[part, :].astype(F32) + dot(straight[part, :], wo_ref[...])
        ).astype(BF16)
        return c

    lax.fori_loop(0, sh.rows // prow, finish, 0)

    def sent(k, c):
        in_copy(k, at_depth(k), d).wait_send()
        out_copy(k, at_depth(k), d).wait_send()
        return c

    lax.fori_loop(1, sh.depth, sent, 0)


def body(sh, alignment, seq_mask, res_mask, rq, rk, rv, ro, cq, ck, cv, co):
    x = alignment.reshape(sh.rows, sh.width)
    spot_marks = jnp.broadcast_to(jnp.tile(res_mask, LANES // sh.spots)[None], (8, LANES))
    seq_marks = jnp.broadcast_to(seq_mask[:, None], (sh.seqs, LANES))
    marks = jnp.stack([spot_marks, seq_marks]).astype(F32)
    vmem = pl.BlockSpec(memory_space=pltpu.VMEM)
    dma = lambda *s: pltpu.SemaphoreType.DMA(s)
    packed = (sh.group, sh.res, sh.spots, sh.wide)
    to_peers = (sh.res, sh.group, sh.spots, sh.wide)
    rows_z = sh.y * sh.block
    down = max(sh.down, 1)
    after, perm, seqs = pl.pallas_call(
        functools.partial(row_kernel, sh),
        out_shape=(
            jax.ShapeDtypeStruct((sh.rows, sh.width), BF16),
            jax.ShapeDtypeStruct((sh.rows, sh.width), BF16),
            jax.ShapeDtypeStruct((sh.depth, 8, LANES), F32),
        ),
        in_specs=[vmem] * 6,
        out_specs=(vmem,) * 3,
        scratch_shapes=[
            pltpu.VMEM((sh.rows, sh.width), BF16),
            pltpu.VMEM(to_peers, BF16),
            pltpu.VMEM(to_peers, BF16),
            pltpu.VMEM(to_peers, BF16),
            pltpu.VMEM(packed, BF16),
            pltpu.VMEM(packed, BF16),
            pltpu.VMEM(packed, BF16),
            pltpu.VMEM((sh.res, 8, LANES), F32),
            pltpu.VMEM((sh.core, sh.tied_rows, sh.half), F32),
            pltpu.VMEM((sh.tied_rows, sh.half), F32),
            pltpu.VMEM((sh.up, rows_z, LANES), F32),
            pltpu.VMEM((down, rows_z, LANES), F32),
            pltpu.VMEM((sh.y, sh.block, LANES), F32),
            pltpu.VMEM((sh.y - 1, sh.block, LANES), F32),
            pltpu.VMEM((sh.y - 1, sh.z, sh.block, LANES), F32),
            pltpu.VMEM((sh.z, sh.block, LANES), F32),
            pltpu.VMEM((sh.z - 1, sh.block, LANES), F32),
            pltpu.VMEM((sh.block, sh.half), F32),
            pltpu.VMEM((sh.block, sh.half), F32),
            pltpu.VMEM((sh.core, sh.tied_rows, sh.half), BF16),
            pltpu.VMEM(packed, BF16),
            pltpu.VMEM(to_peers, BF16),
            pltpu.VMEM((sh.rows, sh.width), BF16),
            dma(sh.depth),
            dma(sh.depth),
            dma(sh.res),
            dma(sh.res),
            dma(3, sh.res),
            dma(3, sh.res),
            dma(4),
            dma(3),
            dma(3),
            dma(sh.up),
            dma(sh.up),
            dma(down),
            dma(down),
            dma(4, sh.y, sh.z),
            dma(4, sh.y, sh.z),
            dma(2, sh.z),
            dma(2, sh.z),
            dma(sh.up),
            dma(sh.up),
            dma(down),
            dma(down),
            dma(sh.res),
            dma(sh.res),
        ],
        compiler_params=pltpu.CompilerParams(
            collective_id=0, has_side_effects=True, vmem_limit_bytes=56 * 2**20
        ),
        name="rows",
    )(x, marks, rq, rk, rv, ro)

    seqs_all = sh.depth * sh.seqs
    message = (sh.depth, sh.msg, sh.width)
    by_spot = (sh.per, seqs_all, sh.width)
    out = pl.pallas_call(
        functools.partial(column_kernel, sh),
        out_shape=jax.ShapeDtypeStruct((sh.rows, sh.width), BF16),
        in_specs=[vmem] * 7,
        out_specs=vmem,
        scratch_shapes=[
            pltpu.VMEM(message, BF16),
            pltpu.VMEM(by_spot, BF16),
            pltpu.VMEM(by_spot, BF16),
            pltpu.VMEM(by_spot, BF16),
            pltpu.VMEM((sh.depth, sh.per, sh.seqs, sh.width), F32),
            pltpu.VMEM(message, BF16),
            pltpu.VMEM(message, BF16),
            pltpu.VMEM((sh.rows, sh.width), BF16),
            dma(sh.depth),
            dma(sh.depth),
            dma(sh.depth),
            dma(sh.depth),
            dma(2),
        ],
        compiler_params=pltpu.CompilerParams(
            collective_id=1, has_side_effects=True, vmem_limit_bytes=56 * 2**20
        ),
        name="columns",
    )(perm.reshape(message), after, seqs, cq, ck, cv, co)
    return out.reshape(alignment.shape)


def build(mesh, sh):
    placed = (P("depth", "res", None), P("depth"), P("res"), P(), P(), P(), P(), P(), P(), P(), P())
    return jax.shard_map(
        functools.partial(body, sh),
        mesh=mesh,
        in_specs=placed,
        out_specs=P("depth", "res", None),
        check_vma=False,
    )


def solution(mesh):
    return build(mesh, Shape())
```

time: 549 us -> 168 us (0.31)
  waiting for transfers between devices: 388 us -> 0 us
  Pallas kernels: 0 us -> 163 us
  blocking collectives: 46.9 us -> 0 us
  matrix products: 41.1 us -> 0 us
  local copies, waits for them, and re-layouts: 34.1 us -> 3.53 us
  starting transfers between devices: 17.4 us -> 0 us
  between operations: 14.1 us -> 0.02 us
    psum x1 -> x0, waiting for transfers between devices: 264 us -> none  [body(): tied = lax.psum(partial_value, 'depth')]
    pallas_call x0 -> x2, Pallas kernels: none -> 163 us  [the longest x1 101 us: body(): pl.pallas_call(functools.partial(row_kernel, sh), out_shape=(jax.ShapeDty...]
    all_gather x2 -> x0, waiting for transfers between devices: 98.9 us -> none  [the longest x1 68 us: body(): lax.all_gather(keys_local, 'res', axis=1, tiled=True)]
    dot_general x11 -> x0, matrix products: 35.5 us -> none  [the longest x1 5.81 us: body(): jnp.einsum('hij,rjhe->rihe', row_weights, value_heads, preferred_element_...]
    all_to_all x1 -> x0, blocking collectives: 28.1 us -> none  [body(): lax.all_to_all(col_mixed, 'depth', split_axis=0, concat_axis=1, tiled=True)]
    all_to_all x2 -> x0, waiting for transfers between devices: 24.5 us -> none  [the longest x1 24.5 us: body(): lax.all_to_all(grouped, 'depth', split_axis=1, concat_axis=0, tiled=True)]
    unnamed x1 -> x0, blocking collectives: 18.8 us -> none
    all_gather x2 -> x0, local copies, waits for them, and re-layouts: 17.4 us -> none  [the longest x1 8.7 us: body(): lax.all_gather(values_local, 'res', axis=1, tiled=True)]
  transfers between devices with their start and end apart: 5 -> 0, of which waited for: 4 -> 0; matrix products, arithmetic and copies ran while one was open for 9% -> 0% of each run, Pallas kernels for 0% -> 0%
where the time goes in v1:
time: 168 us; the launch traced here: 167 us
  Pallas kernels  163 us (97%)
  local copies, waits for them, and re-layouts  3.53 us (2%)
    pallas_call x1, Pallas kernels, body(): pl.pallas_call(functools.partial(row_kernel, sh), out_shape=(jax.ShapeDty...  101 us
    pallas_call x1, Pallas kernels, body(): pl.pallas_call(functools.partial(column_kernel, sh), out_shape=jax.ShapeD...  61.6 us

profile of v1, /device:TPU:2, one launch (start us, length us, event | category | flops | bytes accessed | tf_op | source)
XLA Modules:
  0.0 166.8 jit_solution(17576759412893150174)
XLA Ops:
  0.0 0.7 tile.2
  0.7 0.1 broadcast_in_dim_tile.3
  0.7 0.7 stack_broadcast_in_dim.5
  1.5 0.6 add_convert_fusion.marks_ref
  2.1 101.1 %rows.1 = (bf16[512,768]{1,0:T(8,128)(2,1)}, bf16[512,768]{1,0:T(8,128)(2,1)}, f32[32,8,128]{2,1,0:T(8,128)}) custom-call(bf16[512,768]{1,0:T(8,128)(2,1)} %bitcast.5, f32[2,8,128]{2,1,0:T(8,128)} %add_convert_fusion.marks_ref, bf16[768,768]{1,0:T(8,128)(2,1)} %wq_ref.2, bf16[768,768]{1,0:T(8,128)(2,1)} %wk_ref.2, bf16[768,768]{1,0:T(8,128)(2,1)} %wv_ref.2, ...), custom_call_target="tpu_custom_call" | custom-call | tf_op jit(solution)/shard_map/rows/pallas_call | solution.py:739
  103.2 61.6 %columns.1 = bf16[512,768]{1,0:T(8,128)(2,1)} custom-call(bf16[32,16,768]{2,1,0:T(8,128)(2,1)} %bitcast.4, bf16[512,768]{1,0:T(8,128)(2,1)} %get-tuple-element.9.after_ref, f32[32,8,128]{2,1,0:T(8,128)} %get-tuple-element.10.seqs_ref, bf16[768,768]{1,0:T(8,128)(2,1)} %wq_ref.3, bf16[768,768]{1,0:T(8,128)(2,1)} %wk_ref.3, bf16[768,768]{1,0:T(8,128)(2,1)} %wv_ref.3, ...), custom_call_target="tpu_custom_call" | custom-call | tf_op jit(solution)/shard_map/columns/pallas_call | solution.py:805
  164.7 2.1 %copy.13 = bf16[8,64,768]{2,1,0:T(8,128)(2,1)} copy(bf16[8,64,768]{2,1,0:T(8,128)(2,1)} %bitcast.3) | data formatting | bytes 1572864
  (1 shorter events, 0.0 us)
